TPU v7x, 32 devices: a whole 2x2x4 slice. The times are simulated.
32 devices in a mesh: group: 2 (over y), expert: 4 (over x, core), dp: 4 (over z).
Axes of the slice: x: 2, y: 2, z: 4, core: 2. Of those that a mesh axis runs over, the one named last changes fastest.
Arguments:
- cotangent: bfloat16 [8192, 7168], P(('group', 'expert', 'dp')), parts along dimension 0, may hold values from -6 to 6
- expert_ids: int32 [8192, 8], P(('group', 'expert', 'dp')), parts along dimension 0, may hold values from 0 to 255, all different within a row; in each aligned block of 128 rows (0 to 127, 128 to 255, ...) at most 8 rows name the same one
- gate_values: float32 [8192, 8], P(('group', 'expert', 'dp')), parts along dimension 0, may hold values from 0.02 to 0.3
- hidden: bfloat16 [8, 4, 4, 2, 8, 1024], P(('group', 'expert'), 'dp'), parts along dimension 0, may hold values from -6 to 6
- down_weight: bfloat16 [4, 1024, 7168], P('expert', None, 'dp'), may hold values from -0.1875 to 0.1875
Outputs:
- fisher: float32 [8, 1024, 7168], P(('group', 'expert'), None, 'dp'), parts along dimension 0
- hidden_grad: bfloat16 [8, 4, 4, 2, 8, 1024], P(('group', 'expert'), 'dp'), parts along dimension 0
There are 2 independent parts, one for each index of `group`. A program takes and returns all parts, laid end to end along the dimension named above; an argument that names none is the same for every part. Nothing has to cross between parts.
Inputs may be any that keep to these rules, and one draw needn't show every extreme that they name: `expert_ids`: each token names 8 different experts. In each aligned block of 128 tokens no expert is named by more than 8 tokens, a bound that some block reaches.
All inputs are finite; a program needn't handle non-finite values.
Results may differ from a plain program's by a relative error of at most 0.0051.
Values may be sent and summed in bfloat16 or wider, within the bound.
A program may use at most 128 MiB of HBM per device.

v0:
```python
import jax
import jax.numpy as jnp
from jax import lax
from jax.sharding import PartitionSpec as P

GROUP = 128


def per_device(cotangent, expert_ids, gate_values, hidden, down_weight):
    experts = lax.axis_size("expert")
    ways = lax.axis_size("dp")
    width = cotangent.shape[1]
    capacity = hidden.shape[4]
    groups_dev = hidden.shape[3]
    hidden_units = hidden.shape[5]
    window = jnp.arange(experts, dtype=jnp.int32)
    match = expert_ids[:, :, None] == window[None, None, :]
    chosen = jnp.any(match, axis=1).astype(jnp.int32).reshape(groups_dev, GROUP, experts)
    weight_sel = jnp.sum(jnp.where(match, gate_values[:, :, None], jnp.float32(0.0)), axis=1)
    weight_sel = weight_sel.reshape(groups_dev, GROUP, experts)
    rank = jnp.cumsum(chosen, axis=1) - 1
    slots = jnp.arange(capacity, dtype=jnp.int32)
    place = (rank[..., None] == slots) & (chosen[..., None] == 1)
    slot_gate = jnp.sum(jnp.where(place, weight_sel[..., None], jnp.float32(0.0)), axis=1)
    token_rows = cotangent.reshape(groups_dev, GROUP, width)
    picked = jnp.einsum(
        "jgec,jgd->ejcd", place.astype(jnp.bfloat16), token_rows, preferred_element_type=jnp.float32
    )
    routed = (picked * jnp.transpose(slot_gate, (1, 0, 2))[..., None]).astype(jnp.bfloat16)
    columns = lax.all_to_all(
        lax.all_to_all(routed[None], "expert", split_axis=1, concat_axis=1, tiled=True),
        "dp",
        split_axis=4,
        concat_axis=0,
        tiled=True,
    )
    flat_cols = columns.reshape(-1, columns.shape[4])
    grad_rows = lax.psum_scatter(
        lax.dot_general(
            flat_cols, down_weight[0], (((1,), (1,)), ((), ())), preferred_element_type=jnp.float32
        ),
        "dp",
        scatter_dimension=0,
        tiled=True,
    )
    hidden_grad = grad_rows.astype(jnp.bfloat16).reshape(hidden.shape)
    shard_width = columns.shape[4]
    empty_fisher = jnp.zeros((hidden_units, shard_width), jnp.float32)
    piece = lax.all_gather(hidden, "dp", axis=1, tiled=True)
    count = piece.shape[1]

    def turn(index, accum):
        source = index // groups_dev
        block = index % groups_dev
        block_h = lax.dynamic_index_in_dim(piece[0], source, 0, keepdims=False)
        block_h = lax.dynamic_index_in_dim(block_h, block, 1, keepdims=False).reshape(
            -1, hidden_units
        )
        block_c = lax.dynamic_index_in_dim(columns, source, 0, keepdims=False)
        block_c = lax.dynamic_index_in_dim(block_c, block, 1, keepdims=False).reshape(
            -1, shard_width
        )
        prod = lax.dot_general(
            block_h, block_c, (((0,), (0,)), ((), ())), preferred_element_type=jnp.float32
        )
        return accum + prod * prod

    fisher_sum = lax.fori_loop(0, count * groups_dev, turn, empty_fisher)
    fisher = (fisher_sum * (1.0 / (ways * groups_dev)))[None]
    return (fisher, hidden_grad)


def solution(mesh):
    in_specs = (
        P(("group", "expert", "dp"), None),
        P(("group", "expert", "dp"), None),
        P(("group", "expert", "dp"), None),
        P(("group", "expert"), "dp", None, None, None, None),
        P("expert", None, "dp"),
    )
    out_specs = (
        P(("group", "expert"), None, "dp"),
        P(("group", "expert"), "dp", None, None, None, None),
    )
    return jax.shard_map(
        per_device, mesh=mesh, in_specs=in_specs, out_specs=out_specs, check_vma=False
    )
```

profile of v0, /device:TPU:0, one launch (start us, length us, event | category | flops | bytes accessed | tf_op | source)
XLA Modules:
  0.0 210.9 jit_solution(8177170741901431970)
XLA Ops:
  7.2 0.7 fusion.10
  7.9 0.1 copy.27
  8.1 0.2 reduce_window_sum.11
  8.4 0.7 select_reduce_fusion.1
  9.2 2.6 %fusion.7 = bf16[1,4,2,8,7168]{4,3,1,2,0:T(8,128)(2,1)S(1)} fusion(bf16[2,128,7168,1]{2,1,3,0:T(8,128)(2,1)} %bitcast.49, f32[4,2,8]{2,0,1:T(4,128)S(1)} %bitcast.55, s32[2,128,4]{1,2,0:T(4,128)S(1)} %copy.28, pred[2,128,4]{1,2,0:T(4,128)(4,1)S(1)} %copy.29), kind=kOutput, calls=%fused_computation.9 | convolution fusion | flops 118374400 | bytes 4592896 | tf_op jit(solution)/shard_map/jgec,jgd->ejcd/dot_general | solution.py:26
  11.9 17.1 %all_to_all.23 = bf16[1,4,2,8,7168]{4,3,2,0,1:T(8,128)(2,1)S(1)} all-to-all(bf16[1,4,2,8,7168]{4,3,2,0,1:T(8,128)(2,1)S(1)} %copy.30), channel_id=1, replica_groups=mesh['group'=2,'expert'=4,'dp'=4] {'expert'}, dimensions={1} | all-to-all | bytes 1835008 | tf_op jit(solution)/shard_map/all_to_all | solution.py:31
  29.0 14.6 %copy.31 = bf16[1,4,2,8,7168]{3,1,2,0,4:T(4,128)(2,1)} copy(bf16[1,4,2,8,7168]{4,3,2,0,1:T(8,128)(2,1)S(1)} %all_to_all.23) | data formatting | bytes 1835008 | tf_op jit(solution)/shard_map/all_to_all | solution.py:31
  43.6 18.8 %reshape.79 = bf16[4,2,57344]{2,1,0:T(2,128)(2,1)} reshape(bf16[7168,1,2,4,8]{4,3,2,1,0:T(4,128)(2,1)} %bitcast.47) | data formatting | bytes 1835008
  62.4 4.9 %all-to-all-start.1 = ((bf16[4,2,57344]{2,1,0:T(2,128)(2,1)}), bf16[4,2,57344]{2,1,0:T(2,128)(2,1)S(1)}, u32[]{:S(2)}, u32[]{:S(2)}) async-start(bf16[4,2,57344]{2,1,0:T(2,128)(2,1)} %reshape.79), calls=%async_computation.1 | async-start | bytes 1835008 | tf_op jit(solution)/shard_map/all_to_all | solution.py:30
  67.3 32.4 %all_gather.3 = bf16[1,4,4,2,8,1024]{5,4,3,2,0,1:T(8,128)(2,1)S(1)} all-gather(bf16[1,1,4,2,8,1024]{5,4,3,2,0,1:T(8,128)(2,1)S(1)} %bitcast.53), channel_id=1, replica_groups=mesh['group'=2,'expert'=4,'dp'=4] {'dp'}, dimensions={1}, use_global_device_ids=true | all-gather | bytes 655360 | tf_op jit(solution)/shard_map/all_gather | solution.py:49
  99.7 19.4 %reshape.80 = bf16[7168,1,2,4,8]{4,3,2,1,0:T(4,128)(2,1)} reshape(bf16[4,2,57344]{2,1,0:T(2,128)(2,1)S(1)} %all-to-all-done.1) | data formatting | bytes 1835008
  119.0 17.1 %copy.32 = bf16[1,4,2,8,4,1792]{5,3,2,1,4,0:T(8,128)(2,1)S(1)} copy(bf16[1,4,2,8,4,1792]{3,1,2,5,4,0:T(4,128)(2,1)} %bitcast.48) | data formatting | bytes 1835008 | tf_op jit(solution)/shard_map/all_to_all | solution.py:30
  136.2 4.2 %fusion.8 = f32[256,1024]{1,0:T(8,128)} fusion(bf16[256,1792]{1,0:T(8,128)(2,1)S(1)} %bitcast.50, bf16[1,1024,1792]{2,1,0:T(8,128)(2,1)} %param.11), kind=kOutput, calls=%fused_computation.11 | convolution fusion | flops 939524096 | bytes 5636096 | tf_op jit(solution)/shard_map/dot_general | solution.py:39
  140.4 55.5 %while.17 = (s32[]{:T(128)}, f32[1024,1792]{1,0:T(8,128)}, bf16[1,4,4,2,8,1024]{5,4,3,2,1,0:T(8,128)(2,1)S(1)}, bf16[4,4,2,8,1792]{4,3,2,1,0:T(8,128)(2,1)S(1)},...) while((s32[]{:T(128)}, f32[1024,1792]{1,0:T(8,128)}, ...), condition=%wide.region_5.6_spmd.clone, body=%wide.region_4.5_spmd.clone.sunk | while | flops 122945560 | bytes 14863173 | solution.py:68
  140.4 4.2 %select_add_fusion.2 = f32[1024,1792]{1,0:T(8,128)} fusion(f32[1024,1792]{1,0:T(8,128)} %get-tuple-element.208, pred[]{:T(512)S(6)} %compare.16, bf16[4,4,2,8,1792]{4,3,2,1,0:T(8,128)(2,1)S(1)} %get-tuple-element.220, s32[]{:T(128)S(6)} %select_n.92, s32[]{:T(128)S(6)} %select_n.95, bf16[1,4,4,2,8,1024]{5,4,3,2,1,0:T(8,128)(2,1)S(1)} %get-tuple-element.219), kind=kOutput, calls=%fused_computation.clone.1 | convolution fusion | flops 122945536 | bytes 14862848 | tf_op jit(solution)/shard_map/while/body/eval_jaxpr/dot_general | solution.py:63
  144.6 7.4 %select_add_fusion.2 = f32[1024,1792]{1,0:T(8,128)} fusion(f32[1024,1792]{1,0:T(8,128)} %get-tuple-element.208, pred[]{:T(512)S(6)} %compare.16, bf16[4,4,2,8,1792]{4,3,2,1,0:T(8,128)(2,1)S(1)} %get-tuple-element.220, s32[]{:T(128)S(6)} %select_n.92, s32[]{:T(128)S(6)} %select_n.95, bf16[1,4,4,2,8,1024]{5,4,3,2,1,0:T(8,128)(2,1)S(1)} %get-tuple-element.219), kind=kOutput, calls=%fused_computation.clone.1 | convolution fusion | flops 122945536 | bytes 14862848 | tf_op jit(solution)/shard_map/while/body/eval_jaxpr/dot_general | solution.py:63
  152.1 7.3 %select_add_fusion.2 = f32[1024,1792]{1,0:T(8,128)} fusion(f32[1024,1792]{1,0:T(8,128)} %get-tuple-element.208, pred[]{:T(512)S(6)} %compare.16, bf16[4,4,2,8,1792]{4,3,2,1,0:T(8,128)(2,1)S(1)} %get-tuple-element.220, s32[]{:T(128)S(6)} %select_n.92, s32[]{:T(128)S(6)} %select_n.95, bf16[1,4,4,2,8,1024]{5,4,3,2,1,0:T(8,128)(2,1)S(1)} %get-tuple-element.219), kind=kOutput, calls=%fused_computation.clone.1 | convolution fusion | flops 122945536 | bytes 14862848 | tf_op jit(solution)/shard_map/while/body/eval_jaxpr/dot_general | solution.py:63
  159.4 7.3 %select_add_fusion.2 = f32[1024,1792]{1,0:T(8,128)} fusion(f32[1024,1792]{1,0:T(8,128)} %get-tuple-element.208, pred[]{:T(512)S(6)} %compare.16, bf16[4,4,2,8,1792]{4,3,2,1,0:T(8,128)(2,1)S(1)} %get-tuple-element.220, s32[]{:T(128)S(6)} %select_n.92, s32[]{:T(128)S(6)} %select_n.95, bf16[1,4,4,2,8,1024]{5,4,3,2,1,0:T(8,128)(2,1)S(1)} %get-tuple-element.219), kind=kOutput, calls=%fused_computation.clone.1 | convolution fusion | flops 122945536 | bytes 14862848 | tf_op jit(solution)/shard_map/while/body/eval_jaxpr/dot_general | solution.py:63
  166.7 7.3 %select_add_fusion.2 = f32[1024,1792]{1,0:T(8,128)} fusion(f32[1024,1792]{1,0:T(8,128)} %get-tuple-element.208, pred[]{:T(512)S(6)} %compare.16, bf16[4,4,2,8,1792]{4,3,2,1,0:T(8,128)(2,1)S(1)} %get-tuple-element.220, s32[]{:T(128)S(6)} %select_n.92, s32[]{:T(128)S(6)} %select_n.95, bf16[1,4,4,2,8,1024]{5,4,3,2,1,0:T(8,128)(2,1)S(1)} %get-tuple-element.219), kind=kOutput, calls=%fused_computation.clone.1 | convolution fusion | flops 122945536 | bytes 14862848 | tf_op jit(solution)/shard_map/while/body/eval_jaxpr/dot_general | solution.py:63
  174.0 7.3 %select_add_fusion.2 = f32[1024,1792]{1,0:T(8,128)} fusion(f32[1024,1792]{1,0:T(8,128)} %get-tuple-element.208, pred[]{:T(512)S(6)} %compare.16, bf16[4,4,2,8,1792]{4,3,2,1,0:T(8,128)(2,1)S(1)} %get-tuple-element.220, s32[]{:T(128)S(6)} %select_n.92, s32[]{:T(128)S(6)} %select_n.95, bf16[1,4,4,2,8,1024]{5,4,3,2,1,0:T(8,128)(2,1)S(1)} %get-tuple-element.219), kind=kOutput, calls=%fused_computation.clone.1 | convolution fusion | flops 122945536 | bytes 14862848 | tf_op jit(solution)/shard_map/while/body/eval_jaxpr/dot_general | solution.py:63
  181.3 7.3 %select_add_fusion.2 = f32[1024,1792]{1,0:T(8,128)} fusion(f32[1024,1792]{1,0:T(8,128)} %get-tuple-element.208, pred[]{:T(512)S(6)} %compare.16, bf16[4,4,2,8,1792]{4,3,2,1,0:T(8,128)(2,1)S(1)} %get-tuple-element.220, s32[]{:T(128)S(6)} %select_n.92, s32[]{:T(128)S(6)} %select_n.95, bf16[1,4,4,2,8,1024]{5,4,3,2,1,0:T(8,128)(2,1)S(1)} %get-tuple-element.219), kind=kOutput, calls=%fused_computation.clone.1 | convolution fusion | flops 122945536 | bytes 14862848 | tf_op jit(solution)/shard_map/while/body/eval_jaxpr/dot_general | solution.py:63
  188.6 7.3 %select_add_fusion.2 = f32[1024,1792]{1,0:T(8,128)} fusion(f32[1024,1792]{1,0:T(8,128)} %get-tuple-element.208, pred[]{:T(512)S(6)} %compare.16, bf16[4,4,2,8,1792]{4,3,2,1,0:T(8,128)(2,1)S(1)} %get-tuple-element.220, s32[]{:T(128)S(6)} %select_n.92, s32[]{:T(128)S(6)} %select_n.95, bf16[1,4,4,2,8,1024]{5,4,3,2,1,0:T(8,128)(2,1)S(1)} %get-tuple-element.219), kind=kOutput, calls=%fused_computation.clone.1 | convolution fusion | flops 122945536 | bytes 14862848 | tf_op jit(solution)/shard_map/while/body/eval_jaxpr/dot_general | solution.py:63
  195.9 6.6 %multiply_bitcast_fusion = f32[1,1024,1792]{2,1,0:T(8,128)} fusion(f32[1024,1792]{1,0:T(8,128)} %get-tuple-element.140), kind=kLoop, calls=%fused_computation.10 | loop fusion | flops 1835008 | bytes 14680064 | tf_op jit(solution)/shard_map/broadcast_in_dim | solution.py:69
  202.5 1.6 convert_element_type.26
  (15 shorter events, 0.3 us)
Async XLA Ops:
  43.6 23.7 %copy-start = (bf16[1,1,4,2,8,1024]{5,4,3,2,1,0:T(8,128)(2,1)S(1)}, bf16[1,1,4,2,8,1024]{5,4,3,2,1,0:T(8,128)(2,1)}, u32[]{:S(2)}) copy-start(bf16[1,1,4,2,8,1024]{5,4,3,2,1,0:T(8,128)(2,1)} %param.10) | copy-start | bytes 393220
  62.4 37.3 %all-to-all-start.1 = ((bf16[4,2,57344]{2,1,0:T(2,128)(2,1)}), bf16[4,2,57344]{2,1,0:T(2,128)(2,1)S(1)}, u32[]{:S(2)}, u32[]{:S(2)}) async-start(bf16[4,2,57344]{2,1,0:T(2,128)(2,1)} %reshape.79), calls=%async_computation.1 | async-start | bytes 1835008 | tf_op jit(solution)/shard_map/all_to_all | solution.py:30
  67.2 135.2 %reduce-scatter.2.cloned.1.call-start = ((), (), s32[]{:S(2)}) async-start(), calls=%async_computation.3 | async-start | bytes 1310720 | tf_op jit(solution)/shard_map/reduce_scatter | solution.py:38
Sparse Core Ops, SparseCore 0:
  140.5 27.8 reduce-scatter.1
where the time goes:
time: 212 us; the launch traced here: 211 us
  local copies, waits for them, and re-layouts  70.2 us (33%)
  matrix products  62.3 us (29%)
  blocking collectives  49.5 us (23%)
  between operations  14.1 us (7%)
  other arithmetic  10 us (5%)
  starting transfers between devices  4.87 us (2%)
    dot_general x8, matrix products, turn(): lax.dot_general(block_h, block_c, (((0,), (0,)), ((), ())), preferred_ele...  55.4 us
    unnamed x4, local copies, waits for them, and re-layouts  38.2 us
    all_gather x1, blocking collectives, per_device(): piece = lax.all_gather(hidden, 'dp', axis=1, tiled=True)  32.4 us
    all_to_all x1, local copies, waits for them, and re-layouts, per_device(): lax.all_to_all(lax.all_to_all(routed[None], 'expert', split_axis=1, conca...  17.1 us
    all_to_all x1, blocking collectives, per_device(): lax.all_to_all(routed[None], 'expert', split_axis=1, concat_axis=1, tiled...  17.1 us
    all_to_all x1, local copies, waits for them, and re-layouts, per_device(): lax.all_to_all(routed[None], 'expert', split_axis=1, concat_axis=1, tiled...  14.6 us
    broadcast_in_dim x1, other arithmetic, per_device(): fisher = (fisher_sum * (1.0 / (ways * groups_dev)))[None]  6.6 us
    all_to_all x1, starting transfers between devices, per_device(): lax.all_to_all(lax.all_to_all(routed[None], 'expert', split_axis=1, conca...  4.87 us
  transfers between devices with their start and end apart: 2, of which 0 were waited for; matrix products, arithmetic and copies ran while one was open for 29% of the time, Pallas kernels for 0%

commit v1 on v0

--- a/solution.py
+++ b/solution.py
@@ -28,7 +28,12 @@
     )
     routed = (picked * jnp.transpose(slot_gate, (1, 0, 2))[..., None]).astype(jnp.bfloat16)
     columns = lax.all_to_all(
-        lax.all_to_all(routed[None], "expert", split_axis=1, concat_axis=1, tiled=True),
+        jnp.concatenate(
+            lax.all_to_all(
+                jnp.stack(jnp.split(routed[None], lax.axis_size("expert"), axis=1)), "expert", 0, 0
+            ),
+            axis=1,
+        ),
         "dp",
         split_axis=4,
         concat_axis=0,

time: 212 us -> 233 us (1.099)
  local copies, waits for them, and re-layouts: 70.2 us -> 90.4 us
    reshape x0 -> x1, local copies, waits for them, and re-layouts: none -> 24 us  [per_device(): jnp.concatenate(lax.all_to_all(jnp.stack(jnp.split(routed[None], lax.axis...]
    all_to_all x2 -> x1, local copies, waits for them, and re-layouts: 31.8 us -> 27.9 us  [per_device(): lax.all_to_all(jnp.concatenate(lax.all_to_all(jnp.stack(jnp.split(routed[...]
  transfers between devices with their start and end apart: 2 -> 2, of which waited for: 0 -> 0; matrix products, arithmetic and copies ran while one was open for 29% -> 27% of each run, Pallas kernels for 0% -> 0%
where the time goes in v1:
time: 233 us; the launch traced here: 231 us
  local copies, waits for them, and re-layouts  90.4 us (39%)
  matrix products  62.3 us (27%)
  blocking collectives  49.5 us (21%)
  between operations  14.1 us (6%)
  other arithmetic  10.1 us (4%)
  starting transfers between devices  4.87 us (2%)
    dot_general x8, matrix products, turn(): lax.dot_general(block_h, block_c, (((0,), (0,)), ((), ())), preferred_ele...  55.4 us
    unnamed x4, local copies, waits for them, and re-layouts  38.2 us
    all_gather x1, blocking collectives, per_device(): piece = lax.all_gather(hidden, 'dp', axis=1, tiled=True)  32.4 us
    all_to_all x1, local copies, waits for them, and re-layouts, per_device(): lax.all_to_all(jnp.concatenate(lax.all_to_all(jnp.stack(jnp.split(routed[...  27.9 us
    reshape x1, local copies, waits for them, and re-layouts, per_device(): jnp.concatenate(lax.all_to_all(jnp.stack(jnp.split(routed[None], lax.axis...  24 us
    all_to_all x1, blocking collectives, per_device(): lax.all_to_all(jnp.stack(jnp.split(routed[None], lax.axis_size('expert'),...  17.1 us
    broadcast_in_dim x1, other arithmetic, per_device(): fisher = (fisher_sum * (1.0 / (ways * groups_dev)))[None]  6.6 us
    all_to_all x1, starting transfers between devices, per_device(): lax.all_to_all(jnp.concatenate(lax.all_to_all(jnp.stack(jnp.split(routed[...  4.87 us
  transfers between devices with their start and end apart: 2, of which 0 were waited for; matrix products, arithmetic and copies ran while one was open for 27% of the time, Pallas kernels for 0%

profile of v1, /device:TPU:0, one launch (start us, length us, event | category | flops | bytes accessed | tf_op | source)
XLA Modules:
  0.0 231.3 jit_solution(12038748967528284239)
XLA Ops:
  7.2 0.7 fusion.10
  7.9 0.1 copy.35
  8.1 0.2 reduce_window_sum.11
  8.4 0.7 select_reduce_fusion.1
  9.2 2.6 %fusion.7 = bf16[1,4,2,8,7168]{4,3,1,2,0:T(8,128)(2,1)S(1)} fusion(bf16[2,128,7168,1]{2,1,3,0:T(8,128)(2,1)} %bitcast.64, f32[4,2,8]{2,0,1:T(4,128)S(1)} %bitcast.71, s32[2,128,4]{1,2,0:T(4,128)S(1)} %copy.36, pred[2,128,4]{1,2,0:T(4,128)(4,1)S(1)} %copy.37), kind=kOutput, calls=%fused_computation.9 | convolution fusion | flops 118374400 | bytes 4592896 | tf_op jit(solution)/shard_map/jgec,jgd->ejcd/dot_general | solution.py:26
  12.0 17.1 %all_to_all.23 = bf16[4,1,1,2,8,7168]{5,4,3,2,1,0:T(8,128)(2,1)S(1)} all-to-all(bf16[4,1,1,2,8,7168]{5,4,3,2,1,0:T(8,128)(2,1)S(1)} %pad_maximum_fusion), channel_id=1, replica_groups=mesh['group'=2,'expert'=4,'dp'=4] {'expert'}, dimensions={0} | all-to-all | bytes 1835008 | tf_op jit(solution)/shard_map/all_to_all | solution.py:32
  29.1 24.0 %copy.41 = bf16[1,4,2,8,7168]{3,2,1,0,4:T(2,128)(2,1)} copy(bf16[1,4,2,8,7168]{4,3,2,1,0:T(8,128)(2,1)S(1)} %bitcast.65) | data formatting | bytes 1835008 | tf_op jit(solution)/shard_map/reshape | solution.py:31
  53.1 18.8 %reshape.83 = bf16[4,2,57344]{2,1,0:T(2,128)(2,1)} reshape(bf16[7168,1,4,2,8]{4,3,2,1,0:T(2,128)(2,1)} %bitcast.62) | data formatting | bytes 1835008
  71.9 4.9 %all-to-all-start.1 = ((bf16[4,2,57344]{2,1,0:T(2,128)(2,1)}), bf16[4,2,57344]{2,1,0:T(2,128)(2,1)S(1)}, u32[]{:S(2)}, u32[]{:S(2)}) async-start(bf16[4,2,57344]{2,1,0:T(2,128)(2,1)} %reshape.83), calls=%async_computation.1 | async-start | bytes 1835008 | tf_op jit(solution)/shard_map/all_to_all | solution.py:30
  76.8 32.4 %all_gather.3 = bf16[1,4,4,2,8,1024]{5,4,3,2,0,1:T(8,128)(2,1)S(1)} all-gather(bf16[1,1,4,2,8,1024]{5,4,3,2,0,1:T(8,128)(2,1)S(1)} %bitcast.69), channel_id=1, replica_groups=mesh['group'=2,'expert'=4,'dp'=4] {'dp'}, dimensions={1}, use_global_device_ids=true | all-gather | bytes 655360 | tf_op jit(solution)/shard_map/all_gather | solution.py:54
  109.2 19.4 %reshape.84 = bf16[7168,1,4,2,8]{4,3,2,1,0:T(2,128)(2,1)} reshape(bf16[4,2,57344]{2,1,0:T(2,128)(2,1)S(1)} %all-to-all-done.1) | data formatting | bytes 1835008
  128.6 27.9 %copy.42 = bf16[1,4,2,8,4,1792]{5,3,2,1,4,0:T(8,128)(2,1)S(1)} copy(bf16[1,4,2,8,4,1792]{3,2,1,5,4,0:T(2,128)(2,1)} %bitcast.63) | data formatting | bytes 1835008 | tf_op jit(solution)/shard_map/all_to_all | solution.py:30
  156.5 4.2 %fusion.8 = f32[256,1024]{1,0:T(8,128)} fusion(bf16[256,1792]{1,0:T(8,128)(2,1)S(1)} %bitcast.66, bf16[1,1024,1792]{2,1,0:T(8,128)(2,1)} %param.11), kind=kOutput, calls=%fused_computation.11 | convolution fusion | flops 939524096 | bytes 5636096 | tf_op jit(solution)/shard_map/dot_general | solution.py:44
  160.7 55.5 %while.17 = (s32[]{:T(128)}, f32[1024,1792]{1,0:T(8,128)}, bf16[1,4,4,2,8,1024]{5,4,3,2,1,0:T(8,128)(2,1)S(1)}, bf16[4,4,2,8,1792]{4,3,2,1,0:T(8,128)(2,1)S(1)},...) while((s32[]{:T(128)}, f32[1024,1792]{1,0:T(8,128)}, ...), condition=%wide.region_5.6_spmd.clone, body=%wide.region_4.5_spmd.clone.sunk | while | flops 122945560 | bytes 14863173 | solution.py:73
  160.7 4.2 %select_add_fusion.2 = f32[1024,1792]{1,0:T(8,128)} fusion(f32[1024,1792]{1,0:T(8,128)} %get-tuple-element.212, pred[]{:T(512)S(6)} %compare.16, bf16[4,4,2,8,1792]{4,3,2,1,0:T(8,128)(2,1)S(1)} %get-tuple-element.224, s32[]{:T(128)S(6)} %select_n.92, s32[]{:T(128)S(6)} %select_n.95, bf16[1,4,4,2,8,1024]{5,4,3,2,1,0:T(8,128)(2,1)S(1)} %get-tuple-element.223), kind=kOutput, calls=%fused_computation.clone.1 | convolution fusion | flops 122945536 | bytes 14862848 | tf_op jit(solution)/shard_map/while/body/eval_jaxpr/dot_general | solution.py:68
  165.0 7.4 %select_add_fusion.2 = f32[1024,1792]{1,0:T(8,128)} fusion(f32[1024,1792]{1,0:T(8,128)} %get-tuple-element.212, pred[]{:T(512)S(6)} %compare.16, bf16[4,4,2,8,1792]{4,3,2,1,0:T(8,128)(2,1)S(1)} %get-tuple-element.224, s32[]{:T(128)S(6)} %select_n.92, s32[]{:T(128)S(6)} %select_n.95, bf16[1,4,4,2,8,1024]{5,4,3,2,1,0:T(8,128)(2,1)S(1)} %get-tuple-element.223), kind=kOutput, calls=%fused_computation.clone.1 | convolution fusion | flops 122945536 | bytes 14862848 | tf_op jit(solution)/shard_map/while/body/eval_jaxpr/dot_general | solution.py:68
  172.4 7.3 %select_add_fusion.2 = f32[1024,1792]{1,0:T(8,128)} fusion(f32[1024,1792]{1,0:T(8,128)} %get-tuple-element.212, pred[]{:T(512)S(6)} %compare.16, bf16[4,4,2,8,1792]{4,3,2,1,0:T(8,128)(2,1)S(1)} %get-tuple-element.224, s32[]{:T(128)S(6)} %select_n.92, s32[]{:T(128)S(6)} %select_n.95, bf16[1,4,4,2,8,1024]{5,4,3,2,1,0:T(8,128)(2,1)S(1)} %get-tuple-element.223), kind=kOutput, calls=%fused_computation.clone.1 | convolution fusion | flops 122945536 | bytes 14862848 | tf_op jit(solution)/shard_map/while/body/eval_jaxpr/dot_general | solution.py:68
  179.7 7.3 %select_add_fusion.2 = f32[1024,1792]{1,0:T(8,128)} fusion(f32[1024,1792]{1,0:T(8,128)} %get-tuple-element.212, pred[]{:T(512)S(6)} %compare.16, bf16[4,4,2,8,1792]{4,3,2,1,0:T(8,128)(2,1)S(1)} %get-tuple-element.224, s32[]{:T(128)S(6)} %select_n.92, s32[]{:T(128)S(6)} %select_n.95, bf16[1,4,4,2,8,1024]{5,4,3,2,1,0:T(8,128)(2,1)S(1)} %get-tuple-element.223), kind=kOutput, calls=%fused_computation.clone.1 | convolution fusion | flops 122945536 | bytes 14862848 | tf_op jit(solution)/shard_map/while/body/eval_jaxpr/dot_general | solution.py:68
  187.0 7.3 %select_add_fusion.2 = f32[1024,1792]{1,0:T(8,128)} fusion(f32[1024,1792]{1,0:T(8,128)} %get-tuple-element.212, pred[]{:T(512)S(6)} %compare.16, bf16[4,4,2,8,1792]{4,3,2,1,0:T(8,128)(2,1)S(1)} %get-tuple-element.224, s32[]{:T(128)S(6)} %select_n.92, s32[]{:T(128)S(6)} %select_n.95, bf16[1,4,4,2,8,1024]{5,4,3,2,1,0:T(8,128)(2,1)S(1)} %get-tuple-element.223), kind=kOutput, calls=%fused_computation.clone.1 | convolution fusion | flops 122945536 | bytes 14862848 | tf_op jit(solution)/shard_map/while/body/eval_jaxpr/dot_general | solution.py:68
  194.4 7.3 %select_add_fusion.2 = f32[1024,1792]{1,0:T(8,128)} fusion(f32[1024,1792]{1,0:T(8,128)} %get-tuple-element.212, pred[]{:T(512)S(6)} %compare.16, bf16[4,4,2,8,1792]{4,3,2,1,0:T(8,128)(2,1)S(1)} %get-tuple-element.224, s32[]{:T(128)S(6)} %select_n.92, s32[]{:T(128)S(6)} %select_n.95, bf16[1,4,4,2,8,1024]{5,4,3,2,1,0:T(8,128)(2,1)S(1)} %get-tuple-element.223), kind=kOutput, calls=%fused_computation.clone.1 | convolution fusion | flops 122945536 | bytes 14862848 | tf_op jit(solution)/shard_map/while/body/eval_jaxpr/dot_general | solution.py:68
  201.6 7.3 %select_add_fusion.2 = f32[1024,1792]{1,0:T(8,128)} fusion(f32[1024,1792]{1,0:T(8,128)} %get-tuple-element.212, pred[]{:T(512)S(6)} %compare.16, bf16[4,4,2,8,1792]{4,3,2,1,0:T(8,128)(2,1)S(1)} %get-tuple-element.224, s32[]{:T(128)S(6)} %select_n.92, s32[]{:T(128)S(6)} %select_n.95, bf16[1,4,4,2,8,1024]{5,4,3,2,1,0:T(8,128)(2,1)S(1)} %get-tuple-element.223), kind=kOutput, calls=%fused_computation.clone.1 | convolution fusion | flops 122945536 | bytes 14862848 | tf_op jit(solution)/shard_map/while/body/eval_jaxpr/dot_general | solution.py:68
  208.9 7.3 %select_add_fusion.2 = f32[1024,1792]{1,0:T(8,128)} fusion(f32[1024,1792]{1,0:T(8,128)} %get-tuple-element.212, pred[]{:T(512)S(6)} %compare.16, bf16[4,4,2,8,1792]{4,3,2,1,0:T(8,128)(2,1)S(1)} %get-tuple-element.224, s32[]{:T(128)S(6)} %select_n.92, s32[]{:T(128)S(6)} %select_n.95, bf16[1,4,4,2,8,1024]{5,4,3,2,1,0:T(8,128)(2,1)S(1)} %get-tuple-element.223), kind=kOutput, calls=%fused_computation.clone.1 | convolution fusion | flops 122945536 | bytes 14862848 | tf_op jit(solution)/shard_map/while/body/eval_jaxpr/dot_general | solution.py:68
  216.2 6.6 %multiply_bitcast_fusion = f32[1,1024,1792]{2,1,0:T(8,128)} fusion(f32[1024,1792]{1,0:T(8,128)} %get-tuple-element.140), kind=kLoop, calls=%fused_computation.10 | loop fusion | flops 1835008 | bytes 14680064 | tf_op jit(solution)/shard_map/broadcast_in_dim | solution.py:74
  222.8 1.6 convert_element_type.26
  (16 shorter events, 0.4 us)
Async XLA Ops:
  53.1 23.7 %copy-start = (bf16[1,1,4,2,8,1024]{5,4,3,2,1,0:T(8,128)(2,1)S(1)}, bf16[1,1,4,2,8,1024]{5,4,3,2,1,0:T(8,128)(2,1)}, u32[]{:S(2)}) copy-start(bf16[1,1,4,2,8,1024]{5,4,3,2,1,0:T(8,128)(2,1)} %param.10) | copy-start | bytes 393220
  71.9 37.3 %all-to-all-start.1 = ((bf16[4,2,57344]{2,1,0:T(2,128)(2,1)}), bf16[4,2,57344]{2,1,0:T(2,128)(2,1)S(1)}, u32[]{:S(2)}, u32[]{:S(2)}) async-start(bf16[4,2,57344]{2,1,0:T(2,128)(2,1)} %reshape.83), calls=%async_computation.1 | async-start | bytes 1835008 | tf_op jit(solution)/shard_map/all_to_all | solution.py:30
  76.8 146.0 %reduce-scatter.2.cloned.1.call-start = ((), (), s32[]{:S(2)}) async-start(), calls=%async_computation.3 | async-start | bytes 1310720 | tf_op jit(solution)/shard_map/reduce_scatter | solution.py:43
Sparse Core Ops, SparseCore 0:
  160.8 27.8 reduce-scatter.1
